TPU v7x, 32 devices: a whole 2x2x4 slice. The times are simulated.
32 devices in a mesh: bead: 16 (over z, x, core), space: 2 (over y).
Axes of the slice: x: 2, y: 2, z: 4, core: 2. Of those that a mesh axis runs over, the one named last changes fastest.
Arguments:
- positions: float32 [16, 3, 1024], P('bead', None, 'space'), may hold values from -6 to 6
- momenta: float32 [16, 3, 1024], P('bead', None, 'space'), may hold values from -6 to 6
- species: int32 [1024], P('space'), may hold values from 0 to 1
- neighbours: int32 [8, 1024], P(None, 'space'), may hold values from 0 to 1023
- send_list: int32 [1024], P('space'), may hold values from 0 to 511
- embedding: float32 [2, 128], replicated, may hold values from -4 to 4
- radial_one: float32 [8, 128], replicated, may hold values from -4 to 4
- radial_two: float32 [8, 128], replicated, may hold values from -4 to 4
- mix_one: float32 [128, 384], replicated, may hold values from -0.3125 to 0.3125
- mix_two: float32 [128, 384], replicated, may hold values from -0.3125 to 0.3125
- read_one: float32 [128], replicated, may hold values from -0.5 to 0.5
- read_two: float32 [128], replicated, may hold values from -0.5 to 0.5
Outputs:
- new_positions: float32 [16, 3, 1024], P('bead', None, 'space')
- new_momenta: float32 [16, 3, 1024], P('bead', None, 'space')
Inputs may be any that keep to these rules, and one draw needn't show every extreme that they name: `neighbours`: positions in the extended set of the atom's own domain: below 256 the ghosts from the lower domain, then the 512 own atoms, then the ghosts from the upper domain. `send_list`: entries d * 512 to d * 512 + 255 are sent to domain d - 1, the next 256 to domain d + 1.
All inputs are finite; a program needn't handle non-finite values.
Results may differ from a plain program's by a relative error of at most 0.0003.
Values sent between devices are 32-bit elements; how exact they have to be, the bound alone decides.
No kernel may reach another device: no remote copies, remote signals or barrier semaphores. Data moves between devices by JAX's collectives and lax.ppermute only.
A program may use at most 128 MiB of HBM per device.

v0:
```python
import math

import jax
import jax.numpy as jnp
from jax import lax
from jax.sharding import PartitionSpec as P

EXACT = lax.Precision.HIGHEST
STEP = 2.0
HALF_STEP = 1.0
HEAVY = 16.0
SQRT3 = math.sqrt(3.0)
SQRT5 = math.sqrt(5.0)
SQRT15 = math.sqrt(15.0)


def padded(cells, sides, width):
    for axis, dim in sides:
        count = lax.axis_size(axis)
        head = lax.slice_in_dim(cells, 0, width, axis=dim)
        tail = lax.slice_in_dim(cells, cells.shape[dim] - width, cells.shape[dim], axis=dim)
        cells = jnp.concatenate(
            [
                lax.ppermute(tail, axis, [(i, (i + 1) % count) for i in range(count)]),
                cells,
                lax.ppermute(head, axis, [((i + 1) % count, i) for i in range(count)]),
            ],
            axis=dim,
        )
    return cells


def harmonics(unit):
    ux, uy, uz = (unit[0], unit[1], unit[2])
    return jnp.stack(
        [
            jnp.ones_like(ux),
            SQRT3 * ux,
            SQRT3 * uy,
            SQRT3 * uz,
            SQRT15 * ux * uy,
            SQRT15 * uy * uz,
            0.5 * SQRT5 * (2.0 * uz * uz - ux * ux - uy * uy),
            SQRT15 * ux * uz,
            0.5 * SQRT15 * (ux * ux - uy * uy),
        ]
    )


def interaction(ext_coords, centre, slots, ext_feat, radial, mixing):
    neigh_count = slots.shape[0]
    atom_count = slots.shape[1]
    flat_slots = slots.reshape(-1)
    relative = (
        jnp.take(ext_coords, flat_slots, axis=1).reshape(3, neigh_count, atom_count)
        - centre[:, None, :]
    )
    soft_dist = jnp.sqrt(jnp.sum(relative * relative, axis=0) + 1.0)
    sphere = harmonics(relative / soft_dist)
    centres = 1.0 + jnp.arange(radial.shape[0]).astype(jnp.float32)
    basis = jnp.exp(-0.5 * (soft_dist[None] - centres[:, None, None]) ** 2)
    edge_weight = jnp.einsum("nc,nka->cka", radial, basis, precision=EXACT)
    carried = edge_weight * jnp.take(ext_feat, flat_slots, axis=1).reshape(
        -1, neigh_count, atom_count
    )
    moments = jnp.einsum("lka,cka->lca", sphere, carried, precision=EXACT) / neigh_count
    squares = moments * moments
    invariants = jnp.concatenate(
        [squares[0], jnp.sum(squares[1:4], axis=0), jnp.sum(squares[4:9], axis=0)], axis=0
    )
    return jnp.dot(mixing, invariants, precision=EXACT)


def embed(embedding, flags):
    return embedding[0][:, None] + flags[None, :] * (embedding[1] - embedding[0])[:, None]


def normal_modes(bead_total):
    bead_idx = jnp.arange(bead_total).astype(jnp.float32)[:, None]
    mode_idx = jnp.arange(bead_total).astype(jnp.float32)[None, :]
    phase = 2.0 * jnp.pi * bead_idx * mode_idx / bead_total
    half_total = bead_total // 2
    table = jnp.where(
        mode_idx < half_total,
        math.sqrt(2.0 / bead_total) * jnp.cos(phase),
        math.sqrt(2.0 / bead_total) * jnp.sin(phase),
    )
    table = jnp.where(
        mode_idx == half_total, jnp.cos(jnp.pi * bead_idx) / math.sqrt(bead_total), table
    )
    table = jnp.where(mode_idx == 0, 1.0 / math.sqrt(bead_total), table)
    return table


def mode_factors(bead_total):
    mode_idx = jnp.arange(bead_total).astype(jnp.float32)
    angles = float(bead_total) * jnp.sin(jnp.pi * mode_idx / bead_total)
    safe_angles = jnp.where(mode_idx == 0, 1.0, angles)
    cosine = jnp.cos(angles)
    reach = jnp.where(mode_idx == 0, STEP, STEP * jnp.sin(angles) / safe_angles)
    stiff = angles * jnp.sin(angles) / STEP
    return (cosine, reach, stiff)


def shards(
    positions,
    momenta,
    species,
    neighbours,
    send_list,
    embedding,
    radial_one,
    radial_two,
    mix_one,
    mix_two,
    read_one,
    read_two,
):
    atoms_here = neighbours.shape[1]
    ghost_rows = atoms_here // 2
    flags = species.astype(jnp.float32)
    masses = HEAVY - (HEAVY - 1.0) * flags
    own_coords = positions[0]
    own_block = jnp.concatenate([own_coords, flags[None, :]], axis=0)
    outgoing = jnp.take(own_block, send_list, axis=1)
    arrived = padded(outgoing, (("space", 1),), ghost_rows)
    extended = jnp.concatenate(
        [arrived[:, :ghost_rows], own_block, arrived[:, -ghost_rows:]], axis=1
    )
    ext_coords = extended[:3]
    base_ext = embed(embedding, extended[3])
    base_own = base_ext[:, ghost_rows : ghost_rows + atoms_here]

    def first_layer(coords_ext):
        centre = coords_ext[:, ghost_rows : ghost_rows + atoms_here]
        return base_own + jax.nn.silu(
            interaction(coords_ext, centre, neighbours, base_ext, radial_one, mix_one)
        )

    hidden_own, first_back = jax.vjp(first_layer, ext_coords)
    feat_out = jnp.take(hidden_own, send_list, axis=1)
    feat_in = padded(feat_out, (("space", 1),), ghost_rows)
    hidden_ext = jnp.concatenate(
        [feat_in[:, :ghost_rows], hidden_own, feat_in[:, -ghost_rows:]], axis=1
    )

    def second_layer(coords_ext, feat_ext):
        centre = coords_ext[:, ghost_rows : ghost_rows + atoms_here]
        top = interaction(coords_ext, centre, neighbours, feat_ext, radial_two, mix_two)
        own_feat = feat_ext[:, ghost_rows : ghost_rows + atoms_here]
        return jnp.sum(jnp.dot(read_two, jax.nn.silu(top), precision=EXACT)) + jnp.sum(
            jnp.dot(read_one, own_feat, precision=EXACT)
        )

    energy_here, second_back = jax.vjp(second_layer, ext_coords, hidden_ext)
    coord_grad_two, feat_grad = second_back(jnp.ones((), jnp.float32))
    feat_ghost = jnp.concatenate(
        [feat_grad[:, :ghost_rows], feat_grad[:, ghost_rows + atoms_here :]], axis=1
    )
    feat_back = padded(feat_ghost, (("space", 1),), ghost_rows)
    feat_recv = jnp.concatenate([feat_back[:, :ghost_rows], feat_back[:, -ghost_rows:]], axis=1)
    hidden_grad = feat_grad[:, ghost_rows : ghost_rows + atoms_here] + jnp.zeros_like(
        hidden_own
    ).at[:, send_list].add(feat_recv)
    (coord_grad_one,) = first_back(hidden_grad)
    coord_grad = coord_grad_one + coord_grad_two
    coord_ghost = jnp.concatenate(
        [coord_grad[:, :ghost_rows], coord_grad[:, ghost_rows + atoms_here :]], axis=1
    )
    coord_back = padded(coord_ghost, (("space", 1),), ghost_rows)
    coord_recv = jnp.concatenate([coord_back[:, :ghost_rows], coord_back[:, -ghost_rows:]], axis=1)
    own_grad = coord_grad[:, ghost_rows : ghost_rows + atoms_here] + jnp.zeros_like(own_coords).at[
        :, send_list
    ].add(coord_recv)
    kicked = momenta[0] - HALF_STEP * own_grad
    bead_total = lax.axis_size("bead")
    my_bead = lax.axis_index("bead")
    modes_mat = normal_modes(bead_total)
    cosine, reach, stiff = mode_factors(bead_total)
    tables = jnp.stack(
        [
            jnp.einsum("jk,k,bk->jb", modes_mat, cosine, modes_mat, precision=EXACT),
            jnp.einsum("jk,k,bk->jb", modes_mat, reach, modes_mat, precision=EXACT),
            jnp.einsum("jk,k,bk->jb", modes_mat, stiff, modes_mat, precision=EXACT),
        ]
    )
    my_row = lax.dynamic_index_in_dim(tables, my_bead, axis=1, keepdims=False)
    coord_piece = lax.all_gather(positions, "bead", axis=0, tiled=True)
    moment_piece = lax.all_gather(kicked[None], "bead", axis=0, tiled=True)
    rotate_q = jnp.einsum("b,bca->ca", my_row[0], coord_piece, precision=EXACT)
    rotate_p = jnp.einsum("b,bca->ca", my_row[0], moment_piece, precision=EXACT)
    drift = jnp.einsum("b,bca->ca", my_row[1], moment_piece, precision=EXACT)
    spring = jnp.einsum("b,bca->ca", my_row[2], coord_piece, precision=EXACT)
    new_coords = rotate_q + drift / masses[None, :]
    new_moms = rotate_p - masses[None, :] * spring
    return (new_coords[None], new_moms[None])


def solution(mesh):
    placed = (
        P("bead", None, "space"),
        P("bead", None, "space"),
        P("space"),
        P(None, "space"),
        P("space"),
        P(),
        P(),
        P(),
        P(),
        P(),
        P(),
        P(),
    )
    return jax.shard_map(
        shards,
        mesh=mesh,
        in_specs=placed,
        out_specs=(P("bead", None, "space"), P("bead", None, "space")),
        check_vma=False,
    )
```

profile of v0, /device:TPU:0, one launch (start us, length us, event | category | flops | bytes accessed | tf_op | source)
XLA Modules:
  0.0 303.8 jit_solution(5044861904998021642)
XLA Ops:
  4.9 3.0 collective-permute-start.1
  8.0 22.4 %all_gather.6 = f32[16,3,512]{2,1,0:T(4,128)S(1)} all-gather(f32[1,3,512]{2,1,0:T(4,128)S(1)} %copy.318), channel_id=1, replica_groups=mesh['bead'=16,'space'=2] {'bead'}, dimensions={0}, use_global_device_ids=true | all-gather | bytes 104448 | tf_op jit(solution)/shard_map/all_gather | solution.py:188
  38.6 10.8 %gather_fusion.4 = f32[4096,3]{1,0:T(8,128)S(1)} fusion(f32[3,1024]{0,1:T(8,128)S(1)} %copy.209, s32[4096]{0:T(1024)S(1)} %get-tuple-element.39), kind=kCustom, calls=%fused_computation.clone | custom fusion | bytes 114688 | tf_op jit(solution)/shard_map/jvp(jit(_take))/gather | solution.py:55
  52.6 14.2 %gather_fusion.1 = f32[4096,128]{1,0:T(8,128)} fusion(f32[128,1024]{0,1:T(8,128)S(1)} %multiply_add_fusion, s32[4096]{0:T(1024)S(1)} %get-tuple-element.56), kind=kCustom, calls=%fused_computation.2 | custom fusion | bytes 4210688 | tf_op jit(solution)/shard_map/jvp(jit(_take))/gather | solution.py:63
  66.9 5.7 %bitcast_multiply_fusion.8 = f32[128,8,512]{0,2,1:T(8,128)S(1)} fusion(f32[128,8,512]{0,2,1:T(8,128)} %bitcast.241, pred[8,512]{1,0:T(8,128)(4,1)S(1)} %compare_and_fusion.1, f32[8]{0:T(128)} %convert_add_fusion, f32[8,512]{1,0:T(8,128)S(1)} %sqrt.17, f32[8,128]{1,0:T(8,128)} %param.20), kind=kOutput, calls=%fused_computation.32 | convolution fusion | flops 51478528 | bytes 4218912 | tf_op jit(solution)/shard_map/jvp(nc,nka->cka)/dot_general | solution.py:62
  73.9 7.4 %fusion.18 = f32[512,128,9]{1,2,0:T(8,128)S(1)} fusion(f32[9,8,512]{0,1,2:T(8,128)S(1)} %copy.212, f32[128,8,512]{0,2,1:T(8,128)S(1)} %bitcast_multiply_fusion.8), kind=kOutput, calls=%fused_computation.39 | convolution fusion | flops 56623104 | bytes 4603904 | tf_op jit(solution)/shard_map/jvp(lka,cka->lca)/dot_general | solution.py:66
  81.6 1.6 copy-done.1
  87.5 2.7 slice_add_fusion
  90.3 2.0 gather_fusion.2
  95.1 3.7 %collective-permute-done.3 = f32[128,256]{0,1:T(8,128)S(1)} collective-permute-done((f32[128,256]{0,1:T(8,128)S(1)}, f32[128,256]{0,1:T(8,128)S(1)}, u32[]{:S(2)}, u32[]{:S(2)}) %collective-permute-start.3) | collective-permute-done | bytes 131104 | tf_op jit(solution)/shard_map/ppermute | solution.py:26
  98.8 2.2 collective-permute-done.2
  102.1 14.2 %gather_fusion.3 = f32[4096,128]{1,0:T(8,128)} fusion(f32[128,1024]{0,1:T(8,128)S(1)} %pad_maximum_fusion, s32[4096]{0:T(1024)S(1)} %get-tuple-element.56), kind=kCustom, calls=%fused_computation.4 | custom fusion | bytes 4210688 | tf_op jit(solution)/shard_map/jvp(jit(_take))/gather | solution.py:63
  116.3 5.7 %bitcast_multiply_fusion.7 = (f32[128,8,512]{0,2,1:T(8,128)S(1)}, f32[8,512,128]{2,1,0:T(8,128)S(1)}) fusion(pred[8,512]{1,0:T(8,128)(4,1)S(1)} %compare_and_fusion.1, f32[4096,128]{1,0:T(8,128)} %gather_fusion.3, f32[8,128]{1,0:T(8,128)S(1)} %copy-done.29, f32[8]{0:T(128)S(1)} %copy-done.33, f32[8,512]{1,0:T(8,128)S(1)} %sqrt.17), kind=kOutput, calls=%fused_computation.31 | convolution fusion | flops 51478528 | bytes 6316064 | tf_op jit(solution)/shard_map/jvp(nc,nka->cka)/dot_general | solution.py:62
  123.3 7.6 %fusion.15 = f32[512,128,9]{1,2,0:T(8,128)S(1)} fusion(f32[9,8,512]{0,1,2:T(8,128)S(1)} %copy.212, f32[128,8,512]{0,2,1:T(8,128)S(1)} %get-tuple-element.48), kind=kOutput, calls=%fused_computation.36 | convolution fusion | flops 56623104 | bytes 4603904 | tf_op jit(solution)/shard_map/jvp(lka,cka->lca)/dot_general | solution.py:66
  135.0 6.8 %fusion.6 = f32[512,128,8]{1,2,0:T(8,128)S(1)} fusion(f32[9,8,512]{0,1,2:T(8,128)S(1)} %copy.212, f32[1,128,512]{1,0,2:T(1,128)S(1)} %bitcast.245, f32[3,128,512]{1,0,2:T(4,128)S(1)} %broadcast_in_dim.213, f32[5,128,512]{1,0,2:T(8,128)S(1)} %broadcast_in_dim.212, f32[512,128,9]{1,2,0:T(8,128)S(1)} %fusion.15), kind=kOutput, calls=%fused_computation.16 | convolution fusion | flops 60162048 | bytes 6963200 | tf_op jit(solution)/shard_map/transpose(jvp(lka,cka->lca))/dot_general | solution.py:66
  141.8 2.0 bitcast_multiply_fusion.5
  143.8 23.0 %scatter_fusion = f32[128,1024]{0,1:T(8,128)S(1)} fusion(f32[128,1024]{0,1:T(8,128)S(1)} %pad.45, s32[4096]{0:T(1024)S(1)} %bitcast.271, f32[4096,128]{1,0:T(8,128)} %bitcast.244), kind=kCustom, calls=%fused_computation.5 | custom fusion | flops 524288 | bytes 6307840 | tf_op jit(solution)/shard_map/transpose(jvp(jit(_take)))/scatter-add | solution.py:63
  167.6 13.6 %fusion.4 = f32[512,9,8]{1,2,0:T(8,128)} fusion(f32[128,8,512]{0,2,1:T(8,128)} %copy-done.8, f32[1,128,512]{1,0,2:T(1,128)S(1)} %bitcast.246, f32[3,128,512]{1,0,2:T(4,128)} %copy-done.13, f32[5,128,512]{1,0,2:T(8,128)} %copy-done.9, f32[512,128,9]{1,2,0:T(8,128)} %copy-done.3), kind=kOutput, calls=%fused_computation.14 | convolution fusion | flops 60162048 | bytes 6963200 | tf_op jit(solution)/shard_map/transpose(jvp(lka,cka->lca))/dot_general | solution.py:66
  181.2 2.9 fusion.34
  186.2 2.2 copy.227
  188.5 2.3 collective-permute-done.5
  192.2 3.6 %scatter_custom_fusion.1 = f32[128,512]{0,1:T(8,128)S(1)} fusion(f32[128,512]{0,1:T(8,128)S(1)} %slice.147, s32[512]{0:T(512)S(1)} %compare_select_fusion.3, f32[128,256]{0,1:T(8,128)S(1)} %collective-permute-done.5, f32[]{:T(128)} %constant.178, f32[128,256]{0,1:T(8,128)S(1)} %collective-permute-done.4), kind=kCustom, calls=%fused_computation.86 | custom fusion | flops 131072 | bytes 524292 | tf_op jit(solution)/shard_map/scatter-add | solution.py:164
  200.1 9.8 %fusion.2 = f32[512,9,8]{1,2,0:T(8,128)} fusion(f32[128,8,512]{0,2,1:T(8,128)S(1)} %copy-done.7, f32[1,128,512]{1,0,2:T(1,128)S(1)} %bitcast.247, f32[3,128,512]{1,0,2:T(4,128)S(1)} %broadcast_in_dim.216, f32[5,128,512]{1,0,2:T(8,128)S(1)} %broadcast_in_dim.215, f32[512,128,9]{1,2,0:T(8,128)S(1)} %copy-done.2), kind=kOutput, calls=%fused_computation.12 | convolution fusion | flops 60162048 | bytes 6963200 | tf_op jit(solution)/shard_map/transpose(jvp(lka,cka->lca))/dot_general | solution.py:66
  209.9 2.3 copy.218
  212.3 8.6 %fusion = f32[512,128,8]{1,2,0:T(8,128)S(1)} fusion(f32[9,8,512]{0,1,2:T(8,128)S(1)} %copy.212, f32[1,128,512]{1,0,2:T(1,128)S(1)} %bitcast.248, f32[3,128,512]{1,0,2:T(4,128)} %copy-done.14, f32[5,128,512]{1,0,2:T(8,128)} %copy-done.10, f32[512,128,9]{1,2,0:T(8,128)} %copy-done.1), kind=kOutput, calls=%fused_computation.10 | convolution fusion | flops 60162048 | bytes 6963200 | tf_op jit(solution)/shard_map/transpose(jvp(lka,cka->lca))/dot_general | solution.py:66
  220.9 2.9 fusion.35
  225.9 2.0 copy.232
  227.9 22.6 %scatter_fusion.1 = f32[3,1024]{0,1:T(8,128)S(1)} fusion(f32[3,1024]{0,1:T(8,128)S(1)} %pad.55, s32[4096]{0:T(1024)S(1)} %get-tuple-element.38, f32[4096,3]{1,0:T(8,128)S(1)} %copy.225), kind=kCustom, calls=%fused_computation.7 | custom fusion | flops 12288 | bytes 163840 | tf_op jit(solution)/shard_map/transpose(jvp(jit(_take)))/scatter-add | solution.py:55
  250.5 22.9 %scatter_fusion.2 = f32[3,1024]{0,1:T(8,128)S(1)} fusion(f32[3,1024]{0,1:T(8,128)S(1)} %pad.59, s32[4096]{0:T(1024)S(1)} %get-tuple-element.38, f32[4096,3]{1,0:T(8,128)} %copy.232), kind=kCustom, calls=%fused_computation.8 | custom fusion | flops 12288 | bytes 163840 | tf_op jit(solution)/shard_map/transpose(jvp(jit(_take)))/scatter-add | solution.py:55
  275.8 3.2 %collective-permute-done.7 = f32[3,256]{0,1:T(8,128)S(1)} collective-permute-done((f32[3,256]{0,1:T(8,128)S(1)}, f32[3,256]{0,1:T(8,128)S(1)}, u32[]{:S(2)}, u32[]{:S(2)}) %collective-permute-start.7) | collective-permute-done | bytes 3104 | tf_op jit(solution)/shard_map/ppermute | solution.py:26
  280.7 3.4 %scatter_fusion.3 = f32[3,512]{0,1:T(8,128)S(1)} fusion(f32[3,512]{0,1:T(8,128)S(1)} %slice.150, s32[512]{0:T(512)S(1)} %compare_select_fusion.3, f32[512,3]{1,0:T(8,128)S(1)} %copy.235), kind=kCustom, calls=%fused_computation.9 | custom fusion | flops 1536 | bytes 20480 | tf_op jit(solution)/shard_map/scatter-add | solution.py:174
  284.2 17.5 %all-gather.1 = f32[16,3,512]{2,1,0:T(4,128)S(1)} all-gather(f32[1,3,512]{2,1,0:T(4,128)S(1)} %copy.236), channel_id=2, replica_groups=mesh['bead'=16,'space'=2] {'bead'}, dimensions={0}, use_global_device_ids=true | all-gather | bytes 104448 | tf_op jit(solution)/shard_map/all_gather | solution.py:189
  (203 shorter events, 46.7 us)
Async XLA Ops:
  0.6 86.9 %copy-start = (f32[128,384]{1,0:T(8,128)S(1)}, f32[128,384]{1,0:T(8,128)}, u32[]{:S(2)}) copy-start(f32[128,384]{1,0:T(8,128)} %param.22) | copy-start | bytes 589828
  0.6 35.5 %copy-start.20 = (s32[8,512]{1,0:T(8,128)S(1)}, s32[8,512]{1,0:T(8,128)}, u32[]{:S(2)}) copy-start(s32[8,512]{1,0:T(8,128)} %param.17) | copy-start | bytes 49156
  0.7 36.8 %copy-start.39 = (f32[128]{0:T(128)S(1)}, f32[128]{0:T(128)}, u32[]{:S(2)}) copy-start(f32[128]{0:T(128)} %param.24) | copy-start | bytes 1540
  2.1 32.5 %copy-start.37 = (pred[512]{0:T(512)(128)(4,1)}, pred[512]{0:T(512)(128)(4,1)S(1)}, u32[]{:S(2)}) copy-start(pred[512]{0:T(512)(128)(4,1)S(1)} %compare_and_fusion.2) | copy-start | bytes 1540
  3.6 32.6 %copy-start.27 = (s32[1024]{0:T(1024)}, s32[1024]{0:T(1024)S(1)}, u32[]{:S(2)}) copy-start(s32[1024]{0:T(1024)S(1)} %pad_clamp_fusion) | copy-start | bytes 12292
  4.9 32.7 %collective-permute-start.1 = (f32[4,256]{0,1:T(8,128)S(1)}, f32[4,256]{0,1:T(8,128)S(1)}, u32[]{:S(2)}, u32[]{:S(2)}) collective-permute-start(f32[4,256]{0,1:T(8,128)S(1)} %get-tuple-element.27), channel_id=1, source_target_pairs={{1,0},{0,1},{3,2},{2,3},{5,4},{4,5},{7,6},{6,7},{9,8},{8,9},{11,10... | collective-permute-start | bytes 12296 | tf_op jit(solution)/shard_map/ppermute | solution.py:26
  7.9 29.7 %collective-permute-start = (f32[4,256]{0,1:T(8,128)S(1)}, f32[4,256]{0,1:T(8,128)S(1)}, u32[]{:S(2)}, u32[]{:S(2)}) collective-permute-start(f32[4,256]{0,1:T(8,128)S(1)} %get-tuple-element.26), channel_id=1, source_target_pairs={{0,1},{1,0},{2,3},{3,2},{4,5},{5,4},{6,7},{7,6},{8,9},{9,8},{10,11... | collective-permute-start | bytes 12296 | tf_op jit(solution)/shard_map/ppermute | solution.py:24
  87.5 4.7 %copy-start.38 = (pred[512]{0:T(512)(128)(4,1)S(1)}, pred[512]{0:T(512)(128)(4,1)}, u32[]{:S(2)}) copy-start(pred[512]{0:T(512)(128)(4,1)} %copy-done.37) | copy-start | bytes 1540
  92.4 6.4 %collective-permute-start.3 = (f32[128,256]{0,1:T(8,128)S(1)}, f32[128,256]{0,1:T(8,128)S(1)}, u32[]{:S(2)}, u32[]{:S(2)}) collective-permute-start(f32[128,256]{0,1:T(8,128)S(1)} %get-tuple-element.25), channel_id=1, source_target_pairs={{1,0},{0,1},{3,2},{2,3},{5,4},{4,5},{7,6},{6,7},{9,8},{8,9},{11,10... | collective-permute-start | bytes 393224 | tf_op jit(solution)/shard_map/ppermute | solution.py:26
  94.0 7.0 %collective-permute-start.2 = (f32[128,256]{0,1:T(8,128)S(1)}, f32[128,256]{0,1:T(8,128)S(1)}, u32[]{:S(2)}, u32[]{:S(2)}) collective-permute-start(f32[128,256]{0,1:T(8,128)S(1)} %get-tuple-element.24), channel_id=1, source_target_pairs={{0,1},{1,0},{2,3},{3,2},{4,5},{5,4},{6,7},{7,6},{8,9},{9,8},{10,11... | collective-permute-start | bytes 393224 | tf_op jit(solution)/shard_map/ppermute | solution.py:24
  102.0 14.2 %copy-start.29 = (f32[8,128]{1,0:T(8,128)S(1)}, f32[8,128]{1,0:T(8,128)}, u32[]{:S(2)}) copy-start(f32[8,128]{1,0:T(8,128)} %param.21) | copy-start | bytes 12292
  102.1 14.2 %copy-start.33 = (f32[8]{0:T(128)S(1)}, f32[8]{0:T(128)}, u32[]{:S(2)}) copy-start(f32[8]{0:T(128)} %convert_add_fusion) | copy-start | bytes 100
  134.8 7.0 %copy-start.13 = (f32[3,128,512]{1,0,2:T(4,128)}, f32[3,128,512]{1,0,2:T(4,128)S(1)}, u32[]{:S(2)}) copy-start(f32[3,128,512]{1,0,2:T(4,128)S(1)} %broadcast_in_dim.213) | copy-start | bytes 2359300
  134.9 6.9 %copy-start.9 = (f32[5,128,512]{1,0,2:T(8,128)}, f32[5,128,512]{1,0,2:T(8,128)S(1)}, u32[]{:S(2)}) copy-start(f32[5,128,512]{1,0,2:T(8,128)S(1)} %broadcast_in_dim.212) | copy-start | bytes 3932164
  167.6 13.6 %copy-start.5 = (f32[512,128,8]{1,2,0:T(8,128)S(1)}, f32[512,128,8]{1,2,0:T(8,128)}, u32[]{:S(2)}) copy-start(f32[512,128,8]{1,2,0:T(8,128)} %copy-done.4) | copy-start | bytes 6291460
  167.6 13.6 %copy-start.12 = (f32[4096,128]{1,0:T(8,128)S(1)}, f32[4096,128]{1,0:T(8,128)}, u32[]{:S(2)}) copy-start(f32[4096,128]{1,0:T(8,128)} %gather_fusion.3) | copy-start | bytes 6291460
  184.1 11.7 %copy-start.17 = (f32[128,512]{0,1:T(8,128)S(1)}, f32[128,512]{0,1:T(8,128)}, u32[]{:S(2)}) copy-start(f32[128,512]{0,1:T(8,128)} %get-tuple-element.47) | copy-start | bytes 786436
  184.1 6.6 %collective-permute-start.5 = (f32[128,256]{0,1:T(8,128)}, f32[128,256]{0,1:T(8,128)S(1)}, u32[]{:S(2)}, u32[]{:S(2)}) collective-permute-start(f32[128,256]{0,1:T(8,128)} %get-tuple-element.23), channel_id=1, source_target_pairs={{1,0},{0,1},{3,2},{2,3},{5,4},{4,5},{7,6},{6,7},{9,8},{8,9},{11,10... | collective-permute-start | bytes 393224 | tf_op jit(solution)/shard_map/ppermute | solution.py:26
  185.7 6.4 %collective-permute-start.4 = (f32[128,256]{0,1:T(8,128)}, f32[128,256]{0,1:T(8,128)S(1)}, u32[]{:S(2)}, u32[]{:S(2)}) collective-permute-start(f32[128,256]{0,1:T(8,128)} %get-tuple-element.22), channel_id=1, source_target_pairs={{0,1},{1,0},{2,3},{3,2},{4,5},{5,4},{6,7},{7,6},{8,9},{9,8},{10,11... | collective-permute-start | bytes 393224 | tf_op jit(solution)/shard_map/ppermute | solution.py:24
  188.4 7.4 %copy-start.15 = (f32[512,9,8]{0,2,1:T(8,128)}, f32[512,9,8]{0,2,1:T(8,128)S(1)}, u32[]{:S(2)}) copy-start(f32[512,9,8]{0,2,1:T(8,128)S(1)} %copy.227) | copy-start | bytes 442372
  188.5 35.4 %copy-start.21 = (f32[1,8,512]{2,1,0:T(8,128)}, f32[1,8,512]{2,1,0:T(8,128)S(1)}, u32[]{:S(2)}) copy-start(f32[1,8,512]{2,1,0:T(8,128)S(1)} %get-tuple-element.30) | copy-start | bytes 49156
  188.5 35.4 %copy-start.22 = (f32[1,8,512]{2,1,0:T(8,128)}, f32[1,8,512]{2,1,0:T(8,128)S(1)}, u32[]{:S(2)}) copy-start(f32[1,8,512]{2,1,0:T(8,128)S(1)} %get-tuple-element.31) | copy-start | bytes 49156
  212.2 8.7 %copy-start.11 = (f32[4096,128]{1,0:T(8,128)S(1)}, f32[4096,128]{1,0:T(8,128)}, u32[]{:S(2)}) copy-start(f32[4096,128]{1,0:T(8,128)} %gather_fusion.1) | copy-start | bytes 6291460
  212.2 8.7 %copy-start.30 = (f32[8,128]{1,0:T(8,128)S(1)}, f32[8,128]{1,0:T(8,128)}, u32[]{:S(2)}) copy-start(f32[8,128]{1,0:T(8,128)} %param.20) | copy-start | bytes 12292
  212.3 8.7 %copy-start.34 = (f32[8]{0:T(128)S(1)}, f32[8]{0:T(128)}, u32[]{:S(2)}) copy-start(f32[8]{0:T(128)} %convert_add_fusion) | copy-start | bytes 100
  227.9 47.7 %copy-start.35 = (s32[512]{0:T(512)S(1)}, s32[512]{0:T(512)}, u32[]{:S(2)}) copy-start(s32[512]{0:T(512)} %param.16) | copy-start | bytes 6148
  227.9 47.7 %copy-start.36 = (f32[1,3,512]{2,0,1:T(1,128)S(1)}, f32[1,3,512]{2,0,1:T(1,128)}, u32[]{:S(2)}) copy-start(f32[1,3,512]{2,0,1:T(1,128)} %param.15) | copy-start | bytes 18436
  273.4 28.3 %copy-start.32 = (f32[3,1,16]{2,1,0:T(1,128)S(1)}, f32[3,1,16]{2,1,0:T(1,128)}, u32[]{:S(2)}) copy-start(f32[3,1,16]{2,1,0:T(1,128)} %copy-done.31) | copy-start | bytes 580
  273.5 28.7 %copy-start.25 = (f32[1,3,512]{2,0,1:T(1,128)S(1)}, f32[1,3,512]{2,0,1:T(1,128)}, u32[]{:S(2)}) copy-start(f32[1,3,512]{2,0,1:T(1,128)} %fusion.84) | copy-start | bytes 18436
  273.5 28.7 %copy-start.26 = (f32[1,3,512]{2,0,1:T(1,128)S(1)}, f32[1,3,512]{2,0,1:T(1,128)}, u32[]{:S(2)}) copy-start(f32[1,3,512]{2,0,1:T(1,128)} %fusion.86) | copy-start | bytes 18436
  273.5 5.5 %collective-permute-start.7 = (f32[3,256]{0,1:T(8,128)S(1)}, f32[3,256]{0,1:T(8,128)S(1)}, u32[]{:S(2)}, u32[]{:S(2)}) collective-permute-start(f32[3,256]{0,1:T(8,128)S(1)} %get-tuple-element.21), channel_id=1, source_target_pairs={{1,0},{0,1},{3,2},{2,3},{5,4},{4,5},{7,6},{6,7},{9,8},{8,9},{11,10... | collective-permute-start | bytes 9224 | tf_op jit(solution)/shard_map/ppermute | solution.py:26
  275.1 5.3 %collective-permute-start.6 = (f32[3,256]{0,1:T(8,128)S(1)}, f32[3,256]{0,1:T(8,128)S(1)}, u32[]{:S(2)}, u32[]{:S(2)}) collective-permute-start(f32[3,256]{0,1:T(8,128)S(1)} %get-tuple-element.20), channel_id=1, source_target_pairs={{0,1},{1,0},{2,3},{3,2},{4,5},{5,4},{6,7},{7,6},{8,9},{9,8},{10,11... | collective-permute-start | bytes 9224 | tf_op jit(solution)/shard_map/ppermute | solution.py:24
  (17 other events, 37.3 us)
where the time goes:
time: 309 us; the launch traced here: 304 us
  other arithmetic  92.5 us (30%)
  matrix products  79 us (26%)
  local copies, waits for them, and re-layouts  66.6 us (22%)
  blocking collectives  39.8 us (13%)
  waiting for transfers between devices  14.1 us (5%)
  starting transfers between devices  9.38 us (3%)
    dot_general x6, matrix products, interaction(): jnp.einsum('lka,cka->lca', sphere, carried, precision=EXACT) / neigh_count  53.9 us
    scatter-add x2, other arithmetic, interaction(): jnp.take(ext_coords, flat_slots, axis=1).reshape(3, neigh_count, atom_count)  45.4 us
    gather x2, local copies, waits for them, and re-layouts, interaction(): jnp.take(ext_feat, flat_slots, axis=1).reshape(-1, neigh_count, atom_count)  28.4 us
    scatter-add x1, other arithmetic, interaction(): jnp.take(ext_feat, flat_slots, axis=1).reshape(-1, neigh_count, atom_count)  23 us
    all_gather x1, blocking collectives, shards(): coord_piece = lax.all_gather(positions, 'bead', axis=0, tiled=True)  22.4 us
    all_gather x1, blocking collectives, shards(): moment_piece = lax.all_gather(kicked[None], 'bead', axis=0, tiled=True)  17.5 us
    dot_general x4, matrix products, interaction(): edge_weight = jnp.einsum('nc,nka->cka', radial, basis, precision=EXACT)  17.2 us
    gather x2, local copies, waits for them, and re-layouts, interaction(): jnp.take(ext_coords, flat_slots, axis=1).reshape(3, neigh_count, atom_count)  11.4 us
  transfers between devices with their start and end apart: 8, of which 6 were waited for; matrix products, arithmetic and copies ran while one was open for 3% of the time, Pallas kernels for 0%

commit v1 on v0

v1 whole, which is shorter than its diff:
```python
import functools
import math

import jax
import jax.numpy as jnp
import numpy as np
from jax import lax
from jax.experimental import pallas as pl
from jax.experimental.pallas import tpu as pltpu
from jax.sharding import PartitionSpec as P

STEP = 2.0
HALF_STEP = 1.0
HEAVY = 16.0
SQRT3 = math.sqrt(3.0)
SQRT5 = math.sqrt(5.0)
SQRT15 = math.sqrt(15.0)
LANES = 128
ORDERS = 9
GROUP = (0, 1, 1, 1, 2, 2, 2, 2, 2)
HEAD = 8
VMEM_BYTES = 56 * 1024 * 1024
f32 = jnp.float32
bf16 = jnp.bfloat16
HIGH = lax.Precision.HIGH


def split(x):
    hi = x.astype(bf16)
    return hi, (x - hi.astype(f32)).astype(bf16)


def split_rows(x):
    hi = x.astype(bf16).astype(f32)
    return jnp.concatenate([hi, x - hi], axis=0)


def dot(a, b, precision=None):
    return jnp.dot(a, b, preferred_element_type=f32, precision=precision)


def dot_nt(a, b):
    return lax.dot_general(a, b, (((1,), (1,)), ((), ())), preferred_element_type=f32)


def row(x, rows=8):
    return jnp.broadcast_to(x, (rows, x.shape[1]))


def lookup(chunks, wanted, position):
    out = None
    for number, chunk in chunks:
        got = jnp.take_along_axis(row(chunk), position, axis=1, mode="promise_in_bounds")
        out = got if out is None else jnp.where(wanted == number, got, out)
    return out


def harmonics(ux, uy, uz):
    return [
        None,
        SQRT3 * ux,
        SQRT3 * uy,
        SQRT3 * uz,
        SQRT15 * ux * uy,
        SQRT15 * uy * uz,
        0.5 * SQRT5 * (2.0 * uz * uz - ux * ux - uy * uy),
        SQRT15 * ux * uz,
        0.5 * SQRT15 * (ux * ux - uy * uy),
    ]


def silu_parts(v):
    gate = 1.0 / (1.0 + jnp.exp(-v))
    return v * gate, gate * (1.0 + v * (1.0 - gate))


def force_kernel(plan, *refs):
    atoms, near, wide, before, after = plan
    n_wide = len(wide)
    blocks = refs[:n_wide]
    emb_ref, rad1_ref, rad2_ref, mix1_ref, mix2_ref, read1_ref, read2_ref = refs[n_wide : n_wide + 7]
    grad_ref = refs[n_wide + 7]
    (
        geo_ref, y_ref, yb_ref, bk_ref, bt_ref, gidx_ref, as_ref, m1_ref, sp1_ref, hs_ref, oh_ref,
        hj_ref, w_ref, car_ref, m2_ref, inv_ref, dinv_ref, p_ref, dhe_ref, dw_ref, da_ref, q_ref,
        val_ref, ohlo_ref,
    ) = refs[n_wide + 8 :]
    chan = emb_ref.shape[1]
    bases = rad1_ref.shape[0]
    slots = gidx_ref.shape[0]
    n_near = len(near) * atoms
    tiles = atoms // LANES
    half = atoms // 2
    half_tiles = half // LANES
    edges = slots * atoms
    top_rows = val_ref.shape[0] // 6

    emb0 = emb_ref[0:1, :]
    emb_d = emb_ref[1:2, :] - emb0
    rr = jnp.concatenate([rad1_ref[...] * emb0, rad1_ref[...] * emb_d], axis=0) * (1.0 / slots)
    rr_hi = rr.astype(bf16).astype(f32)
    rr_lo = rr - rr_hi
    r2 = rad2_ref[...] * (1.0 / slots)
    r2_hi = r2.astype(bf16).astype(f32)
    r2_lo = r2 - r2_hi
    zeros = jnp.zeros((8, chan), f32)
    turned1 = jnp.concatenate([rr_hi, rr_hi, rr_lo, rr_lo] + [zeros] * 8, axis=0).T
    sides = jnp.concatenate([emb0, emb_d, read1_ref[...], read2_ref[...], zeros[:4]], axis=0)
    turned2 = jnp.concatenate([r2_hi, r2_hi, r2_lo, r2_lo, sides] + [zeros] * 11, axis=0).T
    rr_cols = turned1[:, : 8 * bases].astype(bf16)
    r2_cols = turned2[:, : 4 * bases].astype(bf16)
    emb0_col = turned2[:, 4 * bases : 4 * bases + 1]
    embd_col = turned2[:, 4 * bases + 1 : 4 * bases + 2]
    read1_col = turned2[:, 4 * bases + 2 : 4 * bases + 3]
    read2_col = turned2[:, 4 * bases + 3 : 4 * bases + 4]
    rr_rows = jnp.concatenate(
        [jnp.concatenate([rr_hi, rr_hi], axis=1), jnp.concatenate([rr_lo, jnp.zeros_like(rr_lo)], axis=1)], axis=0
    ).astype(bf16)
    r2_rows = jnp.concatenate(
        [jnp.concatenate([r2_hi, r2_hi], axis=1), jnp.concatenate([r2_lo, jnp.zeros_like(r2_lo)], axis=1)], axis=0
    ).astype(bf16)
    order_col = lax.broadcasted_iota(jnp.int32, (bases, LANES), 0).astype(f32)

    tables = []
    for quantity in range(4):
        chunks = []
        for g in range(n_wide):
            for t in range(tiles):
                chunks.append((g * tiles + t, blocks[g][quantity : quantity + 1, t * LANES : (t + 1) * LANES]))
        tables.append(chunks)
    for q in range(len(near)):
        ghosts = []
        for t in range(half_tiles):
            ghosts.append(
                (t, blocks[before[q]][4:5, half + t * LANES : half + (t + 1) * LANES] + float(before[q] * atoms))
            )
        for t in range(half_tiles):
            ghosts.append(
                (
                    half_tiles + tiles + t,
                    blocks[after[q]][4:5, t * LANES : (t + 1) * LANES] + float(after[q] * atoms),
                )
            )
        for t in range(tiles):
            cols = slice(t * LANES, (t + 1) * LANES)
            here = slice(q * atoms + t * LANES, q * atoms + (t + 1) * LANES)
            slot = blocks[q][HEAD : HEAD + slots, cols].astype(jnp.int32)
            chunk_no = slot >> 7
            far = lookup(ghosts, chunk_no, slot & 127).astype(jnp.int32)
            own = (slot >= half) & (slot < half + atoms)
            gidx = jnp.where(own, slot + (q * atoms - half), far)
            gidx_ref[:, here] = gidx
            chunk_no = gidx >> 7
            place = gidx & 127
            xj, yj, zj, fj = [lookup(tables[i], chunk_no, place) for i in range(4)]
            rx = xj - row(blocks[q][0:1, cols])
            ry = yj - row(blocks[q][1:2, cols])
            rz = zj - row(blocks[q][2:3, cols])
            soft = jnp.sqrt(rx * rx + ry * ry + rz * rz + 1.0)
            back = 1.0 / soft
            ux, uy, uz = rx * back, ry * back, rz * back
            for i, value in enumerate((ux, uy, uz, back, soft, fj)):
                geo_ref[i, :, here] = value
            sphere = harmonics(ux, uy, uz)
            for l in range(1, ORDERS):
                y_ref[l, :, here] = sphere[l]
                if q == 0:
                    for k in range(slots):
                        yb_ref[l, k, :, cols] = row(sphere[l][k : k + 1, :])
            for n in range(bases):
                bk_ref[n, :, here] = jnp.exp(-0.5 * (soft - (1.0 + n)) ** 2)
            for k in range(slots):
                basis = jnp.exp(-0.5 * (row(soft[k : k + 1, :], bases) - (1.0 + order_col)) ** 2)
                bt_ref[k, 0:bases, here] = basis
                bt_ref[k, bases : 2 * bases, here] = basis * row(fj[k : k + 1, :], bases)

    def sums(t, carry):
        here = pl.ds(pl.multiple_of(t * LANES, LANES), LANES)
        low = [None] * ORDERS
        for k in range(slots):
            basis = bt_ref[k, :, here]
            for l in range(ORDERS):
                term = basis if l == 0 else basis * row(y_ref[l, k : k + 1, here], 2 * bases)
                low[l] = term if low[l] is None else low[l] + term
        for l in range(ORDERS):
            both = split_rows(low[l]).astype(bf16)
            as_ref[l, 0 : 4 * bases, here] = both
            as_ref[l, 4 * bases : 8 * bases, here] = both
        return carry

    lax.fori_loop(0, n_near // LANES, sums, 0)

    flags_row = jnp.concatenate([blocks[q][3:4, :] for q in range(len(near))], axis=1)
    wide_cols = 2 * LANES

    def first(j, carry):
        here = pl.ds(pl.multiple_of(j * wide_cols, wide_cols), wide_cols)
        inv = [None, None, None]
        for l in range(ORDERS):
            m = dot(rr_cols, as_ref[l, :, here])
            m1_ref[l, :, here] = m
            inv[GROUP[l]] = m * m if inv[GROUP[l]] is None else inv[GROUP[l]] + m * m
        value = dot(mix1_ref[...], jnp.concatenate(inv, axis=0), HIGH)
        act, slope = silu_parts(value)
        sp1_ref[:, here] = slope
        hidden = act + emb0_col + embd_col * q_ref[0:1, here]
        hi, lo = split(hidden)
        hs_ref[0:chan, here] = hi
        hs_ref[chan : 2 * chan, here] = lo
        return carry

    q_ref[0:1, :] = flags_row
    lax.fori_loop(0, n_near // wide_cols, first, 0)

    def gather(k, carry):
        here = pl.ds(pl.multiple_of(k * atoms, atoms), atoms)
        wanted = gidx_ref[pl.ds(k, 1), 0:atoms]
        for r in range(n_near // LANES):
            ids = lax.broadcasted_iota(jnp.int32, (LANES, atoms), 0) + r * LANES
            oh_ref[r * LANES : (r + 1) * LANES, here] = jnp.where(ids == wanted, 1.0, 0.0).astype(bf16)
        both = dot(hs_ref[...], oh_ref[:, here])
        feat = both[:chan] + both[chan:]
        basis = split_rows(bt_ref[k, 0:bases, 0:atoms])
        weight = dot(r2_cols, jnp.concatenate([basis, basis], axis=0).astype(bf16))
        hj_ref[:, here] = feat
        w_ref[:, here] = weight
        car_ref[:, here] = feat * weight
        return carry

    lax.fori_loop(0, slots, gather, 0)

    pairs = chan // 16

    def moments(step, carry):
        t = step // pairs
        c = step % pairs
        cols = pl.ds(pl.multiple_of(t * LANES, LANES), LANES)
        base = pl.multiple_of(c * 16, 16)
        acc = [[None] * ORDERS, [None] * ORDERS]
        for k in range(slots):
            at = pl.ds(pl.multiple_of(k * atoms + t * LANES, LANES), LANES)
            got = car_ref[pl.ds(base, 16), at]
            for l in range(ORDERS):
                yb = yb_ref[l, k, :, cols] if l else None
                for h in range(2):
                    part = got[8 * h : 8 * h + 8]
                    term = part * yb if l else part
                    acc[h][l] = term if acc[h][l] is None else acc[h][l] + term
        inv = [[None] * 3, [None] * 3]
        for l in range(ORDERS):
            m2_ref[l, pl.ds(base, 16), cols] = jnp.concatenate([acc[0][l], acc[1][l]], axis=0)
            for h in range(2):
                sq = acc[h][l] * acc[h][l]
                g = GROUP[l]
                inv[h][g] = sq if inv[h][g] is None else inv[h][g] + sq
        for g in range(3):
            inv_ref[pl.ds(pl.multiple_of(g * chan + c * 16, 16), 16), cols] = jnp.concatenate(
                [inv[0][g], inv[1][g]], axis=0
            )
        return carry

    lax.fori_loop(0, tiles * pairs, moments, 0)

    for t in range(atoms // wide_cols):
        cols = slice(t * wide_cols, (t + 1) * wide_cols)
        value = dot(mix2_ref[...], inv_ref[:, cols], HIGH)
        _, slope = silu_parts(value)
        slope = slope * (2.0 * read2_col)
        for g in range(3):
            mixed = mix2_ref[:, g * chan : (g + 1) * chan].T
            dinv_ref[g * chan : (g + 1) * chan, cols] = dot(mixed, slope, HIGH)

    k_step = slots // 2

    def back_moments(step, carry):
        t = step // 2
        k0 = (step % 2) * k_step
        cols = pl.ds(pl.multiple_of(t * LANES, LANES), LANES)

        def over(c, acc):
            acc = list(acc)
            base = pl.multiple_of(c * 16, 16)
            dm = []
            scale = [dinv_ref[pl.ds(pl.multiple_of(g * chan + c * 16, 16), 16), cols] for g in range(3)]
            for l in range(ORDERS):
                dm.append(m2_ref[l, pl.ds(base, 16), cols] * scale[GROUP[l]])
            for kk in range(k_step):
                k = k0 + kk
                at = pl.ds(pl.multiple_of(k * atoms + t * LANES, LANES), LANES)
                got = car_ref[pl.ds(base, 16), at]
                out = [dm[0][:8], dm[0][8:]]
                for l in range(1, ORDERS):
                    yb = yb_ref[l, k, :, cols]
                    i = kk * (ORDERS - 1) + l - 1
                    for h in range(2):
                        part = dm[l][8 * h : 8 * h + 8]
                        out[h] = out[h] + part * yb
                        acc[i] = acc[i] + part * got[8 * h : 8 * h + 8]
                dcar = jnp.concatenate(out, axis=0)
                for ref, other in ((dhe_ref, w_ref), (dw_ref, hj_ref)):
                    hi, lo = split(dcar * other[pl.ds(base, 16), at])
                    ref[pl.ds(base, 16), at] = hi
                    ref[pl.ds(pl.multiple_of(chan + c * 16, 16), 16), at] = lo
            return tuple(acc)

        start = tuple(jnp.zeros((8, LANES), f32) for _ in range(k_step * (ORDERS - 1)))
        acc = lax.fori_loop(0, pairs, over, start)
        for kk in range(k_step):
            for l in range(1, ORDERS):
                p_ref[l, pl.ds(pl.multiple_of((k0 + kk) * 8, 8), 8), cols] = acc[kk * (ORDERS - 1) + l - 1]
        return carry

    lax.fori_loop(0, tiles * 2, back_moments, 0)

    for k in range(slots):
        here = slice(k * atoms, (k + 1) * atoms)
        both = dot(r2_rows, dw_ref[:, here])
        dbasis = both[:bases] + both[bases:]
        basis = bt_ref[k, 0:bases, 0:atoms]
        reach = 1.0 + lax.broadcasted_iota(jnp.int32, (bases, atoms), 0).astype(f32)
        p_ref[0, k * 8 : k * 8 + 8, :] = dbasis * basis * (reach - row(geo_ref[4, k : k + 1, 0:atoms], bases))

    def back_first(j, carry):
        start = pl.multiple_of(j * wide_cols, wide_cols)
        here = pl.ds(start, wide_cols)
        both = dot_nt(dhe_ref[...], oh_ref[here, :])
        dh = both[:chan] + both[chan:]
        mine = jnp.where(start < atoms, 1.0, 0.0)
        dtop = (dh + read1_col * mine) * sp1_ref[:, here] * 2.0
        scale = []
        for g in range(3):
            scale.append(dot(mix1_ref[:, g * chan : (g + 1) * chan].T, dtop, HIGH))
        for l in range(ORDERS):
            hi, lo = split(m1_ref[l, :, here] * scale[GROUP[l]])
            out = dot(rr_rows, jnp.concatenate([hi, lo], axis=0))
            da_ref[l, :, here] = out[: 2 * bases] + out[2 * bases :]
        return carry

    lax.fori_loop(0, n_near // wide_cols, back_first, 0)

    lane = lax.broadcasted_iota(jnp.int32, (slots, 16 * slots), 1)
    sub = lax.broadcasted_iota(jnp.int32, (slots, 16 * slots), 0)
    adder = jnp.where(((lane >> 3) & (slots - 1)) == sub, 1.0, 0.0).astype(bf16)
    for l in range(ORDERS):
        q_ref[8 * l : 8 * l + 8, 0:atoms] = dot(adder, split_rows(p_ref[l, :, :]).astype(bf16))

    def back_geometry(t, mine):
        here = pl.ds(pl.multiple_of(t * LANES, LANES), LANES)
        ux, uy, uz, back, soft, fj = [geo_ref[i, :, here] for i in range(6)]
        dy = [None] * ORDERS
        ds = None
        for n in range(bases):
            basis = bk_ref[n, :, here]
            db = None
            for l in range(ORDERS):
                g = row(da_ref[l, n : n + 1, here]) + fj * row(da_ref[l, bases + n : bases + n + 1, here])
                if l:
                    dy[l] = g * basis if dy[l] is None else dy[l] + g * basis
                    db = db + g * y_ref[l, :, here]
                else:
                    db = g
            db = db * basis * ((1.0 + n) - soft)
            ds = db if ds is None else ds + db
        if mine:
            ds = ds + q_ref[0:8, here]
            for l in range(1, ORDERS):
                dy[l] = dy[l] + q_ref[8 * l : 8 * l + 8, here]
        dux = SQRT3 * dy[1] + SQRT15 * (uy * dy[4] + uz * dy[7] + ux * dy[8]) - SQRT5 * ux * dy[6]
        duy = SQRT3 * dy[2] + SQRT15 * (ux * dy[4] + uz * dy[5] - uy * dy[8]) - SQRT5 * uy * dy[6]
        duz = SQRT3 * dy[3] + SQRT15 * (uy * dy[5] + ux * dy[7]) + 2.0 * SQRT5 * uz * dy[6]
        along = ds - (ux * dux + uy * duy + uz * duz) * back
        dr = [dux * back + along * ux, duy * back + along * uy, duz * back + along * uz]
        for i in range(3):
            geo_ref[i, :, here] = dr[i]
        return dr

    def mine_tile(t, carry):
        back_geometry(t, True)
        return carry

    def other_tile(t, carry):
        back_geometry(t, False)
        return carry

    lax.fori_loop(0, tiles, mine_tile, 0)
    lax.fori_loop(tiles, n_near // LANES, other_tile, 0)

    def place_tile(t, carry):
        here = pl.ds(pl.multiple_of(t * LANES, LANES), LANES)
        gidx = gidx_ref[:, here]
        chunk_no = gidx >> 7
        place = gidx & 127
        parts = []
        for i in range(3):
            value = geo_ref[i, :, here]
            hi = value.astype(bf16).astype(f32)
            parts.append((hi, value - hi))
        chunk_ids = lax.broadcasted_iota(jnp.int32, (top_rows, LANES), 0)
        place_ids = lax.broadcasted_iota(jnp.int32, (LANES, LANES), 0)
        for k in range(slots):
            at = pl.ds(pl.multiple_of(k * n_near + t * LANES, LANES), LANES)
            hit = chunk_ids == row(chunk_no[k : k + 1, :], top_rows)
            for i in range(3):
                both = [jnp.where(hit, row(part[k : k + 1, :], top_rows), 0.0) for part in parts[i]]
                val_ref[2 * i * top_rows : 2 * (i + 1) * top_rows, at] = jnp.concatenate(both, axis=0).astype(bf16)
            ohlo_ref[:, at] = jnp.where(place_ids == row(place[k : k + 1, :], LANES), 1.0, 0.0).astype(bf16)
        return carry

    lax.fori_loop(0, n_near // LANES, place_tile, 0)
    landed = dot_nt(val_ref[...], ohlo_ref[...])
    for i in range(3):
        total = (
            landed[2 * i * top_rows : (2 * i + 1) * top_rows] + landed[(2 * i + 1) * top_rows : (2 * i + 2) * top_rows]
        )
        for g in range(n_wide):
            for t in range(tiles):
                line = total[g * tiles + t : g * tiles + t + 1, :]
                if g < len(near):
                    here = slice(g * atoms + t * LANES, g * atoms + (t + 1) * LANES)
                    line = line - jnp.sum(geo_ref[i, :, here], axis=0, keepdims=True)
                grad_ref[g, i : i + 1, t * LANES : (t + 1) * LANES] = line


def ring_plan(domains, atoms):
    near = list(dict.fromkeys(o % domains for o in (0, 1, -1)))
    wide = list(dict.fromkeys(near + [o % domains for o in (2, -2)]))
    before = tuple(wide.index((o - 1) % domains) for o in near)
    after = tuple(wide.index((o + 1) % domains) for o in near)
    return atoms, tuple(near), tuple(wide), before, after


def forces(plan, blocks, embedding, radial_one, radial_two, mix_one, mix_two, read_one, read_two):
    atoms, near, wide, _, _ = plan
    chan = embedding.shape[1]
    bases = radial_one.shape[0]
    slots = blocks[0].shape[0] - HEAD
    n_near = len(near) * atoms
    edges = slots * atoms
    top_rows = -(-len(wide) * atoms // LANES // 8) * 8
    vmem = pl.BlockSpec(memory_space=pltpu.VMEM)
    return pl.pallas_call(
        functools.partial(force_kernel, plan),
        out_shape=jax.ShapeDtypeStruct((len(wide), 3, atoms), f32),
        in_specs=[vmem] * (len(wide) + 7),
        out_specs=vmem,
        scratch_shapes=[
            pltpu.VMEM((6, slots, n_near), f32),
            pltpu.VMEM((ORDERS, slots, n_near), f32),
            pltpu.VMEM((ORDERS, slots, 8, atoms), f32),
            pltpu.VMEM((bases, slots, n_near), f32),
            pltpu.VMEM((slots, 2 * bases, n_near), f32),
            pltpu.VMEM((slots, n_near), jnp.int32),
            pltpu.VMEM((ORDERS, 8 * bases, n_near), bf16),
            pltpu.VMEM((ORDERS, chan, n_near), f32),
            pltpu.VMEM((chan, n_near), f32),
            pltpu.VMEM((2 * chan, n_near), bf16),
            pltpu.VMEM((n_near, edges), bf16),
            pltpu.VMEM((chan, edges), f32),
            pltpu.VMEM((chan, edges), f32),
            pltpu.VMEM((chan, edges), f32),
            pltpu.VMEM((ORDERS, chan, atoms), f32),
            pltpu.VMEM((3 * chan, atoms), f32),
            pltpu.VMEM((3 * chan, atoms), f32),
            pltpu.VMEM((ORDERS, 8 * slots, atoms), f32),
            pltpu.VMEM((2 * chan, edges), bf16),
            pltpu.VMEM((2 * chan, edges), bf16),
            pltpu.VMEM((ORDERS, 2 * bases, n_near), f32),
            pltpu.VMEM((8 * ORDERS, n_near), f32),
            pltpu.VMEM((6 * top_rows, slots * n_near), bf16),
            pltpu.VMEM((LANES, slots * n_near), bf16),
        ],
        compiler_params=pltpu.CompilerParams(vmem_limit_bytes=VMEM_BYTES),
        name="forces",
    )(*blocks, embedding, radial_one, radial_two, mix_one, mix_two, read_one[None], read_two[None])


def mode_tables(bead_total):
    bead = np.arange(bead_total, dtype=np.float64)[:, None]
    mode = np.arange(bead_total, dtype=np.float64)[None, :]
    phase = 2.0 * np.pi * bead * mode / bead_total
    half_total = bead_total // 2
    table = math.sqrt(2.0 / bead_total) * np.where(mode < half_total, np.cos(phase), np.sin(phase))
    table = np.where(mode == half_total, np.cos(np.pi * bead) / math.sqrt(bead_total), table)
    table = np.where(mode == 0, 1.0 / math.sqrt(bead_total), table)
    angles = bead_total * np.sin(np.pi * mode[0] / bead_total)
    safe = np.where(mode[0] == 0, 1.0, angles)
    reach = np.where(mode[0] == 0, STEP, STEP * np.sin(angles) / safe)
    stiff = angles * np.sin(angles) / STEP
    turns = [(table * factor[None, :]) @ table.T for factor in (np.cos(angles), reach, stiff)]
    return np.stack(turns, axis=1).astype(np.float32)


def step_kernel(table_ref, gathered_ref, species_ref, q_ref, p_ref):
    bead_total = gathered_ref.shape[0]
    sums = [None] * 4
    for b in range(bead_total):
        coord = gathered_ref[b, 0:3, :]
        moment = gathered_ref[b, 3:6, :]
        for i, (weight, value) in enumerate(((0, coord), (0, moment), (1, moment), (2, coord))):
            term = table_ref[weight, b] * value
            sums[i] = term if sums[i] is None else sums[i] + term
    mass = HEAVY - (HEAVY - 1.0) * species_ref[...].astype(f32)
    q_ref[0] = sums[0] + sums[2] / mass
    p_ref[0] = sums[1] - mass * sums[3]


def shards(
    positions, momenta, species, neighbours, send_list, embedding, radial_one, radial_two, mix_one, mix_two,
    read_one, read_two,
):
    atoms = neighbours.shape[1]
    domains = lax.axis_size("space")
    plan = ring_plan(domains, atoms)
    wide = plan[2]
    block = jnp.concatenate(
        [
            positions[0],
            species.astype(f32)[None],
            send_list.astype(f32)[None],
            jnp.zeros((HEAD - 5, atoms), f32),
            neighbours.astype(f32),
        ],
        axis=0,
    )
    blocks = [block]
    for offset in wide[1:]:
        blocks.append(lax.ppermute(block, "space", [(i, (i - offset) % domains) for i in range(domains)]))
    grads = forces(plan, blocks, embedding, radial_one, radial_two, mix_one, mix_two, read_one, read_two)
    grad = grads[0]
    for g, offset in enumerate(wide):
        if g:
            grad = grad + lax.ppermute(grads[g], "space", [(i, (i + offset) % domains) for i in range(domains)])
    kicked = momenta[0] - HALF_STEP * grad
    bead_total = lax.axis_size("bead")
    tables = jnp.asarray(mode_tables(bead_total))
    my_table = lax.dynamic_index_in_dim(tables, lax.axis_index("bead"), axis=0, keepdims=False)
    mine = jnp.concatenate([positions[0], kicked], axis=0)
    gathered = lax.all_gather(mine[None], "bead", axis=0, tiled=True)
    vmem = pl.BlockSpec(memory_space=pltpu.VMEM)
    return pl.pallas_call(
        step_kernel,
        out_shape=(jax.ShapeDtypeStruct((1, 3, atoms), f32),) * 2,
        in_specs=[pl.BlockSpec(memory_space=pltpu.SMEM), vmem, vmem],
        out_specs=(vmem, vmem),
        name="step",
    )(my_table, gathered, species[None])


def solution(mesh):
    placed = (
        P("bead", None, "space"),
        P("bead", None, "space"),
        P("space"),
        P(None, "space"),
        P("space"),
        P(),
        P(),
        P(),
        P(),
        P(),
        P(),
        P(),
    )
    return jax.shard_map(
        shards,
        mesh=mesh,
        in_specs=placed,
        out_specs=(P("bead", None, "space"), P("bead", None, "space")),
        check_vma=False,
    )
```

time: 309 us -> 68.9 us (0.22); the launches traced: 304 us -> 68.5 us
  other arithmetic: 92.5 us -> 0.72 us
  matrix products: 79 us -> 0 us
  local copies, waits for them, and re-layouts: 66.6 us -> 5.29 us
  Pallas kernels: 0 us -> 30 us
  blocking collectives: 39.8 us -> 24.4 us
  waiting for transfers between devices: 14.1 us -> 2.26 us
  starting transfers between devices: 9.38 us -> 5.06 us
    dot_general x21 -> x0, matrix products: 79 us -> none  [the longest x6 53.9 us: interaction(): jnp.einsum('lka,cka->lca', sphere, carried, precision=EXACT) / neigh_count]
    scatter-add x5 -> x0, other arithmetic: 75.5 us -> none  [the longest x2 45.4 us: interaction(): jnp.take(ext_coords, flat_slots, axis=1).reshape(3, neigh_count, atom_count)]
    gather x6 -> x0, local copies, waits for them, and re-layouts: 42.8 us -> none  [the longest x2 28.4 us: interaction(): jnp.take(ext_feat, flat_slots, axis=1).reshape(-1, neigh_count, atom_count)]
    pallas_call x0 -> x2, Pallas kernels: none -> 30 us  [the longest x1 28.4 us: forces(): pl.pallas_call(functools.partial(force_kernel, plan), out_shape=jax.Shape...]
    all_gather x2 -> x1, blocking collectives: 39.8 us -> 24.4 us  [shards(): gathered = lax.all_gather(mine[None], 'bead', axis=0, tiled=True)]
    ppermute x8 -> x2, waiting for transfers between devices: 14.1 us -> 2.26 us  [the longest x1 1.89 us: shards(): lax.ppermute(block, 'space', [(i, (i - offset) % domains) for i in range(...]
    unnamed x92 -> x15, local copies, waits for them, and re-layouts: 9.13 us -> 1.32 us
    reduce_sum x7 -> x0, other arithmetic: 5.9 us -> none  [the longest x2 2.17 us: interaction(): jnp.sum(squares[1:4], axis=0)]
  transfers between devices with their start and end apart: 8 -> 2, of which waited for: 6 -> 2; matrix products, arithmetic and copies ran while one was open for 3% -> 2% of each run, Pallas kernels for 0% -> 0%
where the time goes in v1:
time: 68.9 us; the launch traced here: 68.5 us
  Pallas kernels  30 us (44%)
  blocking collectives  24.4 us (35%)
  local copies, waits for them, and re-layouts  5.29 us (8%)
  starting transfers between devices  5.06 us (7%)
  waiting for transfers between devices  2.26 us (3%)
  other arithmetic  0.72 us (1%)
  between operations  0.69 us (1%)
    pallas_call x1, Pallas kernels, forces(): pl.pallas_call(functools.partial(force_kernel, plan), out_shape=jax.Shape...  28.4 us
    all_gather x1, blocking collectives, shards(): gathered = lax.all_gather(mine[None], 'bead', axis=0, tiled=True)  24.4 us
    ppermute x1, starting transfers between devices, shards(): lax.ppermute(block, 'space', [(i, (i - offset) % domains) for i in range(...  3.03 us
    ppermute x1, starting transfers between devices, shards(): lax.ppermute(grads[g], 'space', [(i, (i + offset) % domains) for i in ran...  2.03 us
    pallas_call x2, local copies, waits for them, and re-layouts, shards(): pl.pallas_call(step_kernel, out_shape=(jax.ShapeDtypeStruct((1, 3, atoms)...  1.91 us
    ppermute x1, waiting for transfers between devices, shards(): lax.ppermute(block, 'space', [(i, (i - offset) % domains) for i in range(...  1.89 us
    pallas_call x1, Pallas kernels, shards(): pl.pallas_call(step_kernel, out_shape=(jax.ShapeDtypeStruct((1, 3, atoms)...  1.65 us
  transfers between devices with their start and end apart: 2, of which 2 were waited for; matrix products, arithmetic and copies ran while one was open for 2% of the time, Pallas kernels for 0%

profile of v1, /device:TPU:0, one launch (start us, length us, event | category | flops | bytes accessed | tf_op | source)
XLA Modules:
  0.0 68.5 jit_solution(16565975464020530802)
XLA Ops:
  0.6 0.0 copy-start.4
  0.6 0.0 copy-start.3
  0.7 0.7 %convert_element_type.10 = f32[512]{0:T(512)S(1)} convert(s32[512]{0:T(512)} %param.17) | non-fusion elementwise | flops 512 | bytes 4096 | tf_op jit(solution)/shard_map/convert_element_type | solution.py:519
  1.3 0.0 copy-done.4
  1.4 0.7 %copy.23 = f32[1,3,512]{2,1,0:T(4,128)S(1)} copy(f32[1,3,512]{2,0,1:T(1,128)} %param.13) | data formatting | bytes 12288
  2.0 0.0 copy-done.3
  2.1 0.0 copy-start
  2.1 3.0 %collective-permute-start = (f32[16,512]{1,0:T(8,128)S(1)}, f32[16,512]{1,0:T(8,128)S(1)}, u32[]{:S(2)}, u32[]{:S(2)}) collective-permute-start(f32[16,512]{1,0:T(8,128)S(1)} %concatenate.6.refs_0_), channel_id=1, source_target_pairs={{0,1},{1,0},{2,3},{3,2},{4,5},{5,4},{6,7},{7,6},{8,9},{9,8},{10,11... | collective-permute-start | bytes 98312 | tf_op jit(solution)/shard_map/ppermute | solution.py:527
  5.1 1.9 %collective-permute-done.refs_1_ = f32[16,512]{1,0:T(8,128)S(1)} collective-permute-done((f32[16,512]{1,0:T(8,128)S(1)}, f32[16,512]{1,0:T(8,128)S(1)}, u32[]{:S(2)}, u32[]{:S(2)}) %collective-permute-start) | collective-permute-done | bytes 32800 | tf_op jit(solution)/shard_map/ppermute | solution.py:527
  7.0 0.0 copy-start.2
  7.0 0.0 copy-done
  7.0 0.6 copy-done.2
  7.6 0.0 copy-start.6
  7.6 28.4 %forces.1 = f32[2,3,512]{2,1,0:T(4,128)} custom-call(f32[16,512]{1,0:T(8,128)} %copy-done, f32[16,512]{1,0:T(8,128)} %copy-done.2, f32[2,128]{1,0:T(2,128)} %refs_2_.1, f32[8,128]{1,0:T(8,128)} %refs_3_.1, f32[8,128]{1,0:T(8,128)} %refs_4_.1, f32[128,384]{1,0:T(8,128)} %refs_5_.1, f32[128,384]{1,0:T(8,128)} %refs_6_.1, f32[1,128]{1,0:T(1,128)} %bitcast.27, ...), custom_call_target="tpu_custom_call" | custom-call | tf_op jit(solution)/shard_map/forces/pallas_call | solution.py:441
  36.0 0.0 copy-start.1
  36.0 0.8 %slice_bitcast_fusion = f32[3,512]{1,0:T(4,128)S(1)} fusion(f32[2,3,512]{2,1,0:T(4,128)} %forces.1), kind=kLoop, calls=%fused_computation.1 | loop fusion | bytes 12288 | tf_op jit(solution)/shard_map/squeeze | solution.py:532
  36.8 2.0 %collective-permute-start.1 = (f32[3,512]{1,0:T(4,128)S(1)}, f32[3,512]{1,0:T(4,128)S(1)}, u32[]{:S(2)}, u32[]{:S(2)}) collective-permute-start(f32[3,512]{1,0:T(4,128)S(1)} %slice_bitcast_fusion), channel_id=1, source_target_pairs={{0,1},{1,0},{2,3},{3,2},{4,5},{5,4},{6,7},{7,6},{8,9},{9,8},{10,11... | collective-permute-start | bytes 18440 | tf_op jit(solution)/shard_map/ppermute | solution.py:532
  38.8 1.3 %dynamic-slice_bitcast_fusion.table_ref = f32[3,16]{1,0:T(4,128)} fusion(f32[16,3,16]{2,1,0:T(4,128)} %constant.16.clone, s32[]{:T(128)S(6)} %select_n.4), kind=kLoop, calls=%fused_computation.6 | loop fusion | bytes 388 | tf_op jit(solution)/shard_map/jit(dynamic_index_in_dim)/squeeze | solution.py:536
  40.1 0.4 collective-permute-done.1
  40.5 0.0 copy-done.6
  40.5 0.0 copy-done.1
  40.5 24.4 %all-gather.1.gathered_ref = f32[16,6,512]{2,1,0:T(8,128)} all-gather(f32[1,6,512]{2,1,0:T(8,128)S(1)} %maximum_bitcast_fusion), channel_id=2, replica_groups=mesh['bead'=16,'space'=2] {'bead'}, dimensions={0}, use_global_device_ids=true | all-gather | bytes 208896 | tf_op jit(solution)/shard_map/all_gather | solution.py:538
  64.9 1.6 %step.1 = (f32[1,3,512]{2,1,0:T(4,128)}, f32[1,3,512]{2,1,0:T(4,128)}) custom-call(f32[3,16]{1,0:T(4,128)} %dynamic-slice_bitcast_fusion.table_ref, f32[16,6,512]{2,1,0:T(8,128)} %all-gather.1.gathered_ref, s32[1,512]{1,0:T(1,128)} %bitcast.24), custom_call_target="tpu_custom_call" | custom-call | tf_op jit(solution)/shard_map/step/pallas_call | solution.py:540
  66.6 0.0 copy-start.5
  66.6 1.3 %copy.17 = f32[1,3,512]{2,0,1:T(1,128)} copy(f32[1,3,512]{2,1,0:T(4,128)} %get-tuple-element.4) | data formatting | bytes 12288 | tf_op jit(solution)/shard_map/step/pallas_call | solution.py:540
  67.9 0.0 copy-done.5
  67.9 0.6 copy.18
  (6 shorter events, 0.1 us)
Async XLA Ops:
  0.6 0.7 %copy-start.4 = (s32[512]{0:T(512)S(1)}, s32[512]{0:T(512)}, u32[]{:S(2)}) copy-start(s32[512]{0:T(512)} %param.15) | copy-start | bytes 6148
  0.6 1.4 %copy-start.3 = (s32[8,512]{1,0:T(8,128)S(1)}, s32[8,512]{1,0:T(8,128)}, u32[]{:S(2)}) copy-start(s32[8,512]{1,0:T(8,128)} %param.16) | copy-start | bytes 49156
  2.1 4.9 %copy-start = (f32[16,512]{1,0:T(8,128)}, f32[16,512]{1,0:T(8,128)S(1)}, u32[]{:S(2)}) copy-start(f32[16,512]{1,0:T(8,128)S(1)} %concatenate.6.refs_0_) | copy-start | bytes 98308
  2.1 4.9 %collective-permute-start = (f32[16,512]{1,0:T(8,128)S(1)}, f32[16,512]{1,0:T(8,128)S(1)}, u32[]{:S(2)}, u32[]{:S(2)}) collective-permute-start(f32[16,512]{1,0:T(8,128)S(1)} %concatenate.6.refs_0_), channel_id=1, source_target_pairs={{0,1},{1,0},{2,3},{3,2},{4,5},{5,4},{6,7},{7,6},{8,9},{9,8},{10,11... | collective-permute-start | bytes 98312 | tf_op jit(solution)/shard_map/ppermute | solution.py:527
  7.0 0.6 copy-start.2
  7.6 32.8 %copy-start.6 = (f32[1,3,512]{2,0,1:T(1,128)S(1)}, f32[1,3,512]{2,0,1:T(1,128)}, u32[]{:S(2)}) copy-start(f32[1,3,512]{2,0,1:T(1,128)} %param.14) | copy-start | bytes 18436
  36.0 4.4 %copy-start.1 = (f32[2,3,512]{2,1,0:T(4,128)S(1)}, f32[2,3,512]{2,1,0:T(4,128)}, u32[]{:S(2)}) copy-start(f32[2,3,512]{2,1,0:T(4,128)} %forces.1) | copy-start | bytes 36868
  36.8 3.7 %collective-permute-start.1 = (f32[3,512]{1,0:T(4,128)S(1)}, f32[3,512]{1,0:T(4,128)S(1)}, u32[]{:S(2)}, u32[]{:S(2)}) collective-permute-start(f32[3,512]{1,0:T(4,128)S(1)} %slice_bitcast_fusion), channel_id=1, source_target_pairs={{0,1},{1,0},{2,3},{3,2},{4,5},{5,4},{6,7},{7,6},{8,9},{9,8},{10,11... | collective-permute-start | bytes 18440 | tf_op jit(solution)/shard_map/ppermute | solution.py:532
  66.6 1.3 %copy-start.5 = (f32[1,3,512]{2,1,0:T(4,128)S(1)}, f32[1,3,512]{2,1,0:T(4,128)}, u32[]{:S(2)}) copy-start(f32[1,3,512]{2,1,0:T(4,128)} %get-tuple-element.5) | copy-start | bytes 18436
